TPU v7x, 256 devices: a whole 4x4x8 slice. The times are simulated.
256 devices in a mesh: sector: 8 (over z), rows: 32 (over x, y, core).
Axes of the slice: x: 4, y: 4, z: 8, core: 2. Of those that a mesh axis runs over, the one named last changes fastest.
Arguments:
- x_block: bfloat16 [8, 40960, 300], P('sector', 'rows')
- h_diag: bfloat16 [8, 40960, 1280], P('sector', 'rows')
- h_right: bfloat16 [8, 40960, 1280], P('sector', 'rows')
- pattern: int32 [8, 2, 320, 10], P('sector', None, 'rows'), may hold values from 0 to 1, as said below
Outputs:
- q_block: bfloat16 [8, 40960, 300], P('sector', 'rows')
- hproj: float32 [8, 300, 300], P('sector')
- correlation: float32 [8, 300, 300], P('sector')
Inputs may be any that keep to these rules, and one draw needn't show every extreme that they name: Within each 1280 x 1280 tile, pattern[s, 0] is symmetric with ones on its diagonal; h_diag's tiles are symmetric.
All inputs are finite; a program needn't handle non-finite values.
Results may differ from a plain program's by a relative error of at most 0.011.
Values may be sent and summed in bfloat16 or wider, within the bound.
A program may use at most 64 MiB of HBM per device.

v0:
```python
import jax
import jax.numpy as jnp
from jax import lax
from jax.sharding import PartitionSpec as P

SUBBLOCK = 128


def from_behind(value, axis, steps):
    count = lax.axis_size(axis)
    leading, last = (max(0, -steps), min(count, count - steps))
    return lax.ppermute(value, axis, [(source, source + steps) for source in range(leading, last)])


def column_product(left, right):
    return lax.dot_general(
        left, right, (((0,), (0,)), ((), ())), preferred_element_type=jnp.float32
    )


def expand(blocks):
    return jnp.repeat(jnp.repeat(blocks, SUBBLOCK, axis=0), SUBBLOCK, axis=1)


def apply_factor(rows_b, inverse):
    return jnp.dot(rows_b.astype(jnp.float32), inverse.T, precision=lax.Precision.HIGH).astype(
        jnp.bfloat16
    )


def shards(x_block, h_diag, h_right, pattern):
    inputs = x_block[0]
    masks = pattern[0].astype(jnp.bfloat16)
    diag_tile = h_diag[0] * expand(masks[0])
    right_tile = h_right[0] * expand(masks[1])
    later_rows = from_behind(inputs, "rows", -1)
    carried = column_product(right_tile, inputs)
    earlier = from_behind(carried.astype(jnp.bfloat16), "rows", 1).astype(carried.dtype)
    image = jnp.dot(diag_tile, inputs, preferred_element_type=jnp.float32)
    image = image + jnp.dot(right_tile, later_rows, preferred_element_type=jnp.float32) + earlier
    image_b = image.astype(jnp.bfloat16)
    total_rows = lax.axis_size("rows") * inputs.shape[0]
    gram, rayleigh = lax.psum(
        (column_product(image_b, image_b), column_product(inputs, image_b)), "rows"
    )
    gram = gram / total_rows
    rayleigh = rayleigh / total_rows
    factor = jnp.linalg.cholesky(gram)
    inverse = jax.scipy.linalg.solve_triangular(
        factor, jnp.eye(gram.shape[0], dtype=jnp.float32), lower=True
    )
    basis = apply_factor(image_b, inverse)
    previous = from_behind(basis, "sector", 1)
    correlation = (
        lax.psum(column_product(previous, basis).astype(jnp.bfloat16), "rows").astype(jnp.float32)
        / total_rows
    )
    return (basis[None], rayleigh[None], correlation[None])


def solution(mesh):
    in_specs = (
        P("sector", "rows", None),
        P("sector", "rows", None),
        P("sector", "rows", None),
        P("sector", None, "rows", None),
    )
    out_specs = (P("sector", "rows", None), P("sector", None, None), P("sector", None, None))
    return jax.shard_map(shards, mesh=mesh, in_specs=in_specs, out_specs=out_specs, check_vma=False)
```

profile of v0, /device:TPU:1, one launch (start us, length us, event | category | flops | bytes accessed | tf_op | source)
XLA Modules:
  0.0 392.8 jit_solution(5937771413376753806)
XLA Ops:
  8.2 4.0 %copy.16 = bf16[1,1280,1280]{1,2,0:T(8,128)(2,1)S(1)} copy(bf16[1,1280,1280]{2,1,0:T(8,128)(2,1)} %param.6) | data formatting | bytes 6553600 | tf_op args[2]
  12.4 3.2 fusion.6
  15.7 4.6 %collective-permute-start.1 = (bf16[1280,300]{0,1:T(8,128)(2,1)}, bf16[1280,300]{0,1:T(8,128)(2,1)}, u32[]{:S(2)}, u32[]{:S(2)}) collective-permute-start(bf16[1280,300]{0,1:T(8,128)(2,1)} %fusion.6), channel_id=1, source_target_pairs={{0,1},{1,2},{2,3},{3,4},{4,5},{5,6},{6,7},{7,8},{8,9},{9,10},{10,1... | collective-permute-start | bytes 2304008 | tf_op jit(solution)/shard_map/ppermute | solution.py:12
  20.2 2.7 collective-permute-start
  23.0 1.9 bitcast_multiply_fusion.1
  25.1 4.0 %copy.15 = bf16[1,1280,1280]{1,2,0:T(8,128)(2,1)S(1)} copy(bf16[1,1280,1280]{2,1,0:T(8,128)(2,1)} %param.5) | data formatting | bytes 6553600 | tf_op args[1]
  29.4 2.5 fusion.2
  31.9 1.9 collective-permute-done
  33.8 2.7 fusion.5
  36.5 2.5 convolution_bitcast_fusion
  39.0 1.4 fusion.39
  40.7 118.3 %all-reduce.9.cloned.1.call-done = (f32[300,300]{0,1:T(8,128)}, f32[300,300]{0,1:T(8,128)}) async-done(((f32[300,300]{0,1:T(8,128)}, f32[300,300]{0,1:T(8,128)}), (f32[300,300]{0,1:T(8,128)}, f32[300,300]{0,1:T(8,128)})) %all-reduce.9.cloned.1.call-update) | async-done | bytes 720016 | tf_op jit(solution)/shard_map/psum | solution.py:43
  161.4 11.7 %cholesky.78 = f32[128,128]{1,0:T(8,128)S(1)} custom-call(f32[128,128]{1,0:T(8,128)S(1)} %cholesky.198), custom_call_target="Cholesky" | custom-call | tf_op jit(solution)/shard_map/jit(cholesky)/cholesky | solution.py:48
  173.2 9.8 %custom-call.23 = f32[1,128,128]{1,2,0:T(8,128)S(1)} custom-call(f32[1,128,128]{2,1,0:T(8,128)S(1)} %get-tuple-element.33), custom_call_target="InvertDiagBlocksLowerTriangular" | custom-call | tf_op jit(solution)/shard_map/jit(cholesky)/cholesky | solution.py:48
  183.5 11.7 %cholesky.164 = f32[128,128]{1,0:T(8,128)S(1)} custom-call(f32[128,128]{1,0:T(8,128)S(1)} %cholesky.202), custom_call_target="Cholesky" | custom-call | tf_op jit(solution)/shard_map/jit(cholesky)/cholesky | solution.py:48
  195.3 10.0 %custom-call.24 = f32[1,128,128]{1,2,0:T(8,128)S(1)} custom-call(f32[1,128,128]{2,1,0:T(8,128)S(1)} %get-tuple-element.30), custom_call_target="InvertDiagBlocksLowerTriangular" | custom-call | tf_op jit(solution)/shard_map/jit(cholesky)/cholesky | solution.py:48
  205.7 4.0 %cholesky.186 = f32[44,44]{1,0:T(8,128)S(1)} custom-call(f32[44,44]{1,0:T(8,128)S(1)} %convolution_subtract_fusion.3), custom_call_target="Cholesky" | custom-call | tf_op jit(solution)/shard_map/jit(cholesky)/cholesky | solution.py:48
  213.1 4.0 %while.1 = (s32[]{:T(128)}, f32[300,300]{1,0:T(8,128)S(1)}, s32[2,2]{1,0:T(2,128)S(1)}, f32[2,128,128]{2,1,0:T(8,128)S(1)}, s32[]{:T(128)}) while((s32[]{:T(128)}, f32[300,300]{1,0:T(8,128)S(1)}, s32[2,2]{1,0:T(2,128)S(1)}, f32[2,128,128]{2,1,0:T(8,128)S(1)}, s32[]{:T(128)}) %tuple.32), condition=%wide.while_cond, body=%wide.while_body.sunk | while | flops 2 | bytes 131181 | solution.py:49
  213.7 1.4 bitcast_dynamic-update-slice_fusion.2
  215.7 1.4 bitcast_dynamic-update-slice_fusion.2
  217.2 29.5 %custom-call.25 = f32[3,128,128]{1,2,0:T(8,128)S(1)} custom-call(f32[3,128,128]{2,1,0:T(8,128)S(1)} %pad_maximum_fusion), custom_call_target="InvertDiagBlocksLowerTriangular" | custom-call | tf_op jit(solution)/shard_map/jit(_solve_triangular)/triangular_solve | solution.py:49
  249.8 3.2 collective-permute-start.2
  253.0 16.3 %collective-permute-done.2 = bf16[1280,300]{0,1:T(8,128)(2,1)S(1)} collective-permute-done((bf16[1280,300]{0,1:T(8,128)(2,1)S(1)}, bf16[1280,300]{0,1:T(8,128)(2,1)S(1)}, u32[]{:S(2)}, u32[]{:S(2)}) %collective-permute-start.2) | collective-permute-done | bytes 768032 | tf_op jit(solution)/shard_map/ppermute | solution.py:12
  271.9 112.0 %all-reduce.7.cloned.1.call-done = bf16[300,300]{0,1:T(8,128)(2,1)} async-done(((bf16[300,300]{0,1:T(8,128)(2,1)}), bf16[300,300]{0,1:T(8,128)(2,1)}) %all-reduce.7.cloned.1.call-update) | async-done | bytes 180016 | tf_op jit(solution)/shard_map/psum | solution.py:55
  (64 shorter events, 15.7 us)
Async XLA Ops:
  7.2 151.9 %all-reduce.9.cloned.1.call-start = ((), (), s32[]{:S(2)}) async-start(), calls=%async_computation.1 | async-start | bytes 1867776 | tf_op jit(solution)/shard_map/psum | solution.py:43
  15.7 16.3 %collective-permute-start.1 = (bf16[1280,300]{0,1:T(8,128)(2,1)}, bf16[1280,300]{0,1:T(8,128)(2,1)}, u32[]{:S(2)}, u32[]{:S(2)}) collective-permute-start(bf16[1280,300]{0,1:T(8,128)(2,1)} %fusion.6), channel_id=1, source_target_pairs={{0,1},{1,2},{2,3},{3,4},{4,5},{5,6},{6,7},{7,8},{8,9},{9,10},{10,1... | collective-permute-start | bytes 2304008 | tf_op jit(solution)/shard_map/ppermute | solution.py:12
  20.2 13.5 %collective-permute-start = (bf16[1280,300]{0,1:T(8,128)(2,1)}, bf16[1280,300]{0,1:T(8,128)(2,1)}, u32[]{:S(2)}, u32[]{:S(2)}) collective-permute-start(bf16[1280,300]{0,1:T(8,128)(2,1)} %bitcast.3), channel_id=1, source_target_pairs={{1,0},{2,1},{3,2},{4,3},{5,4},{6,5},{7,6},{8,7},{9,8},{10,9},{11,1... | collective-permute-start | bytes 2304008 | tf_op jit(solution)/shard_map/ppermute | solution.py:12
  29.4 4.4 %copy-start = (bf16[1280,1280]{0,1:T(8,128)(2,1)S(1)}, bf16[1280,1280]{0,1:T(8,128)(2,1)}, u32[]{:S(2)}) copy-start(bf16[1280,1280]{0,1:T(8,128)(2,1)} %bitcast_multiply_fusion.1) | copy-start | bytes 9830404
  40.4 343.5 %all-reduce.7.cloned.1.call-start = ((), (), s32[]{:S(2)}) async-start(), calls=%async_computation | async-start | bytes 466944 | tf_op jit(solution)/shard_map/psum | solution.py:55
  217.2 53.5 %copy-start.2 = (f32[300,300]{0,1:T(8,128)S(1)}, f32[300,300]{0,1:T(8,128)}, u32[]{:S(2)}) copy-start(f32[300,300]{0,1:T(8,128)} %get-tuple-element.26) | copy-start | bytes 1080004
  249.7 136.2 %copy-start.1 = (bf16[1280,300]{0,1:T(8,128)(2,1)}, bf16[1280,300]{0,1:T(8,128)(2,1)S(1)}, u32[]{:S(2)}) copy-start(bf16[1280,300]{0,1:T(8,128)(2,1)S(1)} %convolution_convert_fusion) | copy-start | bytes 2304004
  249.8 19.6 %collective-permute-start.2 = (bf16[1280,300]{0,1:T(8,128)(2,1)S(1)}, bf16[1280,300]{0,1:T(8,128)(2,1)S(1)}, u32[]{:S(2)}, u32[]{:S(2)}) collective-permute-start(bf16[1280,300]{0,1:T(8,128)(2,1)S(1)} %convolution_convert_fusion), channel_id=1, source_target_pairs={{0,32},{32,64},{64,96},{96,128},{128,160},{160,192},{192,224},{1,3... | collective-permute-start | bytes 2304008 | tf_op jit(solution)/shard_map/ppermute | solution.py:12
Sparse Core Ops, SparseCore 0:
  40.5 118.5 all-reduce.8
  270.7 113.0 all-reduce.6
where the time goes:
time: 393 us
  waiting for transfers between devices  248 us (63%)
  other arithmetic  84.6 us (22%)
  matrix products  17.4 us (4%)
  between operations  16.4 us (4%)
  local copies, waits for them, and re-layouts  15.1 us (4%)
  starting transfers between devices  10.8 us (3%)
    psum x1, waiting for transfers between devices, shards(): lax.psum((column_product(image_b, image_b), column_product(inputs, image_...  118 us
    psum x1, waiting for transfers between devices, shards(): lax.psum(column_product(previous, basis).astype(jnp.bfloat16), 'rows')  112 us
    another operation x10, other arithmetic, shards(): factor = jnp.linalg.cholesky(gram)  48.6 us
    another operation x7, other arithmetic, shards(): jax.scipy.linalg.solve_triangular(factor, jnp.eye(gram.shape[0], dtype=jn...  29.7 us
    ppermute x3, waiting for transfers between devices, from_behind(): lax.ppermute(value, axis, [(source, source + steps) for source in range(l...  18.2 us
    unnamed x16, local copies, waits for them, and re-layouts  10.7 us
    ppermute x3, starting transfers between devices, from_behind(): lax.ppermute(value, axis, [(source, source + steps) for source in range(l...  10.5 us
    dot_general x4, matrix products, column_product(): lax.dot_general(left, right, (((0,), (0,)), ((), ())), preferred_element_...  8.37 us
  transfers between devices with their start and end apart: 5, of which 4 were waited for; matrix products, arithmetic and copies ran while one was open for 3% of the time, Pallas kernels for 0%

commit v1 on v0

--- a/solution.py
+++ b/solution.py
@@ -52,7 +52,9 @@
     basis = apply_factor(image_b, inverse)
     previous = from_behind(basis, "sector", 1)
     correlation = (
-        lax.psum(column_product(previous, basis).astype(jnp.bfloat16), "rows").astype(jnp.float32)
+        jnp.sum(
+            lax.all_gather(column_product(previous, basis).astype(jnp.bfloat16), "rows"), axis=0
+        ).astype(jnp.float32)
         / total_rows
     )
     return (basis[None], rayleigh[None], correlation[None])

time: 393 us -> 342 us (0.87)
  waiting for transfers between devices: 248 us -> 194 us
    psum x1 -> x0, waiting for transfers between devices: 112 us -> none  [shards(): lax.psum(column_product(previous, basis).astype(jnp.bfloat16), 'rows')]
    all_gather x0 -> x1, waiting for transfers between devices: none -> 57.3 us  [shards(): lax.all_gather(column_product(previous, basis).astype(jnp.bfloat16), 'rows')]
    reduce_sum x0 -> x1, other arithmetic: none -> 4.47 us  [shards(): jnp.sum(lax.all_gather(column_product(previous, basis).astype(jnp.bfloat1...]
where the time goes in v1:
time: 342 us; the launch traced here: 341 us
  waiting for transfers between devices  194 us (57%)
  other arithmetic  88.1 us (26%)
  matrix products  16.9 us (5%)
  between operations  16.4 us (5%)
  local copies, waits for them, and re-layouts  15.3 us (4%)
  starting transfers between devices  10.8 us (3%)
    psum x1, waiting for transfers between devices, shards(): lax.psum((column_product(image_b, image_b), column_product(inputs, image_...  118 us
    all_gather x1, waiting for transfers between devices, shards(): lax.all_gather(column_product(previous, basis).astype(jnp.bfloat16), 'rows')  57.3 us
    another operation x10, other arithmetic, shards(): factor = jnp.linalg.cholesky(gram)  48.6 us
    another operation x7, other arithmetic, shards(): jax.scipy.linalg.solve_triangular(factor, jnp.eye(gram.shape[0], dtype=jn...  29.7 us
    ppermute x3, waiting for transfers between devices, from_behind(): lax.ppermute(value, axis, [(source, source + steps) for source in range(l...  18.2 us
    unnamed x16, local copies, waits for them, and re-layouts  10.7 us
    ppermute x3, starting transfers between devices, from_behind(): lax.ppermute(value, axis, [(source, source + steps) for source in range(l...  10.5 us
    dot_general x4, matrix products, column_product(): lax.dot_general(left, right, (((0,), (0,)), ((), ())), preferred_element_...  8.37 us
  transfers between devices with their start and end apart: 5, of which 4 were waited for; matrix products, arithmetic and copies ran while one was open for 3% of the time, Pallas kernels for 0%

profile of v1, /device:TPU:1, one launch (start us, length us, event | category | flops | bytes accessed | tf_op | source)
XLA Modules:
  0.0 341.4 jit_solution(3297947666557771156)
XLA Ops:
  8.2 4.0 %copy.25 = bf16[1,1280,1280]{1,2,0:T(8,128)(2,1)S(1)} copy(bf16[1,1280,1280]{2,1,0:T(8,128)(2,1)} %param.6) | data formatting | bytes 6553600 | tf_op args[2]
  12.4 3.2 fusion.6
  15.7 4.6 %collective-permute-start.1 = (bf16[1280,300]{0,1:T(8,128)(2,1)}, bf16[1280,300]{0,1:T(8,128)(2,1)}, u32[]{:S(2)}, u32[]{:S(2)}) collective-permute-start(bf16[1280,300]{0,1:T(8,128)(2,1)} %fusion.6), channel_id=1, source_target_pairs={{0,1},{1,2},{2,3},{3,4},{4,5},{5,6},{6,7},{7,8},{8,9},{9,10},{10,1... | collective-permute-start | bytes 2304008 | tf_op jit(solution)/shard_map/ppermute | solution.py:12
  20.2 2.7 collective-permute-start
  23.0 1.9 bitcast_multiply_fusion.1
  25.1 4.0 %copy.24 = bf16[1,1280,1280]{1,2,0:T(8,128)(2,1)S(1)} copy(bf16[1,1280,1280]{2,1,0:T(8,128)(2,1)} %param.5) | data formatting | bytes 6553600 | tf_op args[1]
  29.4 2.5 fusion.2
  31.9 1.9 collective-permute-done
  33.8 2.7 fusion.5
  36.5 2.5 convolution_bitcast_fusion
  40.7 118.3 %all-reduce.6.cloned.1.call-done = (f32[300,300]{0,1:T(8,128)}, f32[300,300]{0,1:T(8,128)}) async-done(((f32[300,300]{0,1:T(8,128)}, f32[300,300]{0,1:T(8,128)}), (f32[300,300]{0,1:T(8,128)}, f32[300,300]{0,1:T(8,128)})) %all-reduce.6.cloned.1.call-update) | async-done | bytes 720016 | tf_op jit(solution)/shard_map/psum | solution.py:43
  161.4 11.7 %cholesky.78 = f32[128,128]{1,0:T(8,128)S(1)} custom-call(f32[128,128]{1,0:T(8,128)S(1)} %cholesky.198), custom_call_target="Cholesky" | custom-call | tf_op jit(solution)/shard_map/jit(cholesky)/cholesky | solution.py:48
  173.2 9.8 %custom-call.23 = f32[1,128,128]{1,2,0:T(8,128)S(1)} custom-call(f32[1,128,128]{2,1,0:T(8,128)S(1)} %get-tuple-element.36), custom_call_target="InvertDiagBlocksLowerTriangular" | custom-call | tf_op jit(solution)/shard_map/jit(cholesky)/cholesky | solution.py:48
  183.6 11.7 %cholesky.164 = f32[128,128]{1,0:T(8,128)S(1)} custom-call(f32[128,128]{1,0:T(8,128)S(1)} %cholesky.202), custom_call_target="Cholesky" | custom-call | tf_op jit(solution)/shard_map/jit(cholesky)/cholesky | solution.py:48
  195.3 10.0 %custom-call.24 = f32[1,128,128]{1,2,0:T(8,128)S(1)} custom-call(f32[1,128,128]{2,1,0:T(8,128)S(1)} %get-tuple-element.33), custom_call_target="InvertDiagBlocksLowerTriangular" | custom-call | tf_op jit(solution)/shard_map/jit(cholesky)/cholesky | solution.py:48
  205.7 4.0 %cholesky.186 = f32[44,44]{1,0:T(8,128)S(1)} custom-call(f32[44,44]{1,0:T(8,128)S(1)} %convolution_subtract_fusion.3), custom_call_target="Cholesky" | custom-call | tf_op jit(solution)/shard_map/jit(cholesky)/cholesky | solution.py:48
  213.1 4.0 %while.1 = (s32[]{:T(128)}, f32[300,300]{1,0:T(8,128)S(1)}, s32[2,2]{1,0:T(2,128)S(1)}, f32[2,128,128]{2,1,0:T(8,128)S(1)}, s32[]{:T(128)}) while((s32[]{:T(128)}, f32[300,300]{1,0:T(8,128)S(1)}, s32[2,2]{1,0:T(2,128)S(1)}, f32[2,128,128]{2,1,0:T(8,128)S(1)}, s32[]{:T(128)}) %tuple.33), condition=%wide.while_cond, body=%wide.while_body.sunk | while | flops 2 | bytes 131181 | solution.py:49
  213.7 1.4 bitcast_dynamic-update-slice_fusion.2
  215.7 1.4 bitcast_dynamic-update-slice_fusion.2
  217.2 29.5 %custom-call.25 = f32[3,128,128]{1,2,0:T(8,128)S(1)} custom-call(f32[3,128,128]{2,1,0:T(8,128)S(1)} %pad_maximum_fusion), custom_call_target="InvertDiagBlocksLowerTriangular" | custom-call | tf_op jit(solution)/shard_map/jit(_solve_triangular)/triangular_solve | solution.py:49
  249.2 3.2 collective-permute-start.2
  252.5 16.3 %collective-permute-done.2 = bf16[1280,300]{0,1:T(8,128)(2,1)S(1)} collective-permute-done((bf16[1280,300]{0,1:T(8,128)(2,1)S(1)}, bf16[1280,300]{0,1:T(8,128)(2,1)S(1)}, u32[]{:S(2)}, u32[]{:S(2)}) %collective-permute-start.2) | collective-permute-done | bytes 768032 | tf_op jit(solution)/shard_map/ppermute | solution.py:12
  271.3 57.3 %all-gather.4.cloned.1.call-done = bf16[32,300,300]{2,1,0:T(8,128)(2,1)} async-done(((bf16[1,300,300]{2,1,0:T(8,128)(2,1)}), bf16[32,300,300]{2,1,0:T(8,128)(2,1)}) %all-gather.4.cloned.1.call-update) | async-done | bytes 5760016 | tf_op jit(solution)/shard_map/all_gather | solution.py:56
  328.7 4.5 %reduce_sum.12 = bf16[300,300]{1,0:T(8,128)(2,1)S(1)} reduce(bf16[32,300,300]{2,1,0:T(8,128)(2,1)} %all-gather.4.cloned.1.call-done, bf16[]{:T(256)} %constant.127.clone.1), dimensions={0}, to_apply=%region_8.9 | reduce | flops 2790000 | bytes 5940002 | tf_op jit(solution)/shard_map/reduce_sum | solution.py:55
  (66 shorter events, 15.8 us)
Async XLA Ops:
  7.2 151.9 %all-reduce.6.cloned.1.call-start = ((), (), s32[]{:S(2)}) async-start(), calls=%async_computation.1 | async-start | bytes 1867776 | tf_op jit(solution)/shard_map/psum | solution.py:43
  15.7 16.3 %collective-permute-start.1 = (bf16[1280,300]{0,1:T(8,128)(2,1)}, bf16[1280,300]{0,1:T(8,128)(2,1)}, u32[]{:S(2)}, u32[]{:S(2)}) collective-permute-start(bf16[1280,300]{0,1:T(8,128)(2,1)} %fusion.6), channel_id=1, source_target_pairs={{0,1},{1,2},{2,3},{3,4},{4,5},{5,6},{6,7},{7,8},{8,9},{9,10},{10,1... | collective-permute-start | bytes 2304008 | tf_op jit(solution)/shard_map/ppermute | solution.py:12
  20.2 13.5 %collective-permute-start = (bf16[1280,300]{0,1:T(8,128)(2,1)}, bf16[1280,300]{0,1:T(8,128)(2,1)}, u32[]{:S(2)}, u32[]{:S(2)}) collective-permute-start(bf16[1280,300]{0,1:T(8,128)(2,1)} %bitcast.3), channel_id=1, source_target_pairs={{1,0},{2,1},{3,2},{4,3},{5,4},{6,5},{7,6},{8,7},{9,8},{10,9},{11,1... | collective-permute-start | bytes 2304008 | tf_op jit(solution)/shard_map/ppermute | solution.py:12
  29.4 4.4 %copy-start = (bf16[1280,1280]{0,1:T(8,128)(2,1)S(1)}, bf16[1280,1280]{0,1:T(8,128)(2,1)}, u32[]{:S(2)}) copy-start(bf16[1280,1280]{0,1:T(8,128)(2,1)} %bitcast_multiply_fusion.1) | copy-start | bytes 9830404
  40.4 288.3 %all-gather.4.cloned.1.call-start = ((), (), s32[]{:S(2)}) async-start(), calls=%async_computation | async-start | bytes 7704576 | tf_op jit(solution)/shard_map/all_gather | solution.py:56
  217.2 52.9 %copy-start.2 = (f32[300,300]{0,1:T(8,128)S(1)}, f32[300,300]{0,1:T(8,128)}, u32[]{:S(2)}) copy-start(f32[300,300]{0,1:T(8,128)} %get-tuple-element.29) | copy-start | bytes 1080004
  249.2 83.9 %copy-start.1 = (bf16[1280,300]{0,1:T(8,128)(2,1)}, bf16[1280,300]{0,1:T(8,128)(2,1)S(1)}, u32[]{:S(2)}) copy-start(bf16[1280,300]{0,1:T(8,128)(2,1)S(1)} %convolution_convert_fusion) | copy-start | bytes 2304004
  249.2 19.6 %collective-permute-start.2 = (bf16[1280,300]{0,1:T(8,128)(2,1)S(1)}, bf16[1280,300]{0,1:T(8,128)(2,1)S(1)}, u32[]{:S(2)}, u32[]{:S(2)}) collective-permute-start(bf16[1280,300]{0,1:T(8,128)(2,1)S(1)} %convolution_convert_fusion), channel_id=1, source_target_pairs={{0,32},{32,64},{64,96},{96,128},{128,160},{160,192},{192,224},{1,3... | collective-permute-start | bytes 2304008 | tf_op jit(solution)/shard_map/ppermute | solution.py:12
Sparse Core Ops, SparseCore 0:
  40.5 118.5 all-reduce.5
  270.2 58.4 all-gather.3
